TPU v7x, 32 devices: a whole 2x2x4 slice. The times are simulated.
32 devices in a mesh: dp: 4 (over y, core), ctx: 8 (over z, x).
Axes of the slice: x: 2, y: 2, z: 4, core: 2. Of those that a mesh axis runs over, the one named last changes fastest.
Arguments:
- feat_clean: bfloat16 [4, 512, 6144], P('dp', 'ctx'), may hold values from -6 to 6
- feat_pert: bfloat16 [4, 512, 6144], P('dp', 'ctx'), may hold values from -6 to 6
- feat_teacher: bfloat16 [4, 512, 6144], P('dp', 'ctx'), may hold values from -6 to 6
- short_taps: float32 [3, 6144], replicated, may hold values from -3 to 3
- residues: float32 [2048, 16], replicated, may hold values from -0.26565564 to 0.26565564
- decay_rate: float32 [2048, 16], replicated, may hold values from 0.0001953125 to 0.0333333333
- out_weight: bfloat16 [2048, 4096], P(None, 'dp'), may hold values from -0.125 to 0.125
- norm_gain: float32 [4096], replicated, may hold values from 0.1 to 1.9
Outputs:
- grad_clean: bfloat16 [4, 512, 6144], P('dp', 'ctx')
- grad_pert: bfloat16 [4, 512, 6144], P('dp', 'ctx')
All inputs are finite; a program needn't handle non-finite values.
Results may differ from a plain program's by a relative error of at most 0.018.
Values may be sent and summed in bfloat16 or wider, within the bound.
A program may use at most 192 MiB of HBM per device.

v0:
```python
import math

import jax
import jax.numpy as jnp
from jax import lax
from jax.sharding import PartitionSpec as P

eps = 1e-06
teacher_weight = 0.5
highest = lax.Precision.HIGHEST


def passed_along(value, axis, steps):
    count = lax.axis_size(axis)
    first, last = (max(0, -steps), min(count, count - steps))
    return lax.ppermute(value, axis, [(source, source + steps) for source in range(first, last)])


def split_table(table):
    upper = table.astype(jnp.bfloat16)
    lower = (table - upper.astype(jnp.float32)).astype(jnp.bfloat16)
    return (upper, lower)


def split_product(form, table, data):
    upper, lower = split_table(table)
    return jnp.einsum(form, upper, data, preferred_element_type=jnp.float32) + jnp.einsum(
        form, lower, data, preferred_element_type=jnp.float32
    )


def modal_group(group_parts):
    group_data, group_res, group_decay_factor = group_parts
    streams, group_width, length = group_data.shape
    block = min(128, length)
    total_block_count = length // block
    positions = jnp.arange(block, dtype=jnp.float32)
    powers = jnp.exp(-group_decay_factor[:, :, None] * positions[None, None, :])
    kernel = jnp.einsum("gm,gmk->gk", group_res, powers, precision=highest)
    offset = jnp.arange(block)[:, None] - jnp.arange(block)[None, :]
    toeplitz = jnp.where(
        offset[None] >= 0, jnp.take(kernel, jnp.clip(offset, 0, block - 1), axis=1), 0.0
    )
    blocks = group_data.reshape(streams, group_width, total_block_count, block)
    within = split_product("gij,sgkj->sgki", toeplitz, blocks)
    tail_decay = jnp.exp(-group_decay_factor[:, :, None] * (block - 1.0 - positions)[None, None, :])
    block_ends = split_product("gmj,sgkj->sgkm", tail_decay, blocks)
    blocks_at = jnp.arange(total_block_count)
    block_lag = (blocks_at[:, None] - 1 - blocks_at[None, :]).astype(jnp.float32)
    carry_map = jnp.where(
        block_lag[None, None] >= 0.0,
        jnp.exp(
            -group_decay_factor[:, :, None, None] * block * jnp.maximum(block_lag, 0.0)[None, None]
        ),
        0.0,
    )
    states = jnp.einsum("gmab,sgbm->sgam", carry_map, block_ends, precision=highest)
    reach_map = group_res[:, :, None] * jnp.exp(
        -group_decay_factor[:, :, None] * (positions + 1.0)[None, None, :]
    )
    between = jnp.einsum("gmi,sgkm->sgki", reach_map, states, precision=highest)
    final_map = jnp.exp(
        -group_decay_factor[:, :, None]
        * block
        * (total_block_count - 1 - blocks_at).astype(jnp.float32)[None, None, :]
    )
    end_state = jnp.einsum("gmk,sgkm->sgm", final_map, block_ends, precision=highest)
    return ((within + between).reshape(streams, group_width, length), end_state)


def modal_conv(signal, residues, decay_rate):
    streams, channels, length = signal.shape
    group_width = math.gcd(channels, 64)
    groups = channels // group_width
    grouped = signal.reshape(streams, groups, group_width, length).transpose(1, 0, 2, 3)
    result, end_state = lax.map(
        modal_group,
        (
            grouped,
            residues.reshape(groups, group_width, -1),
            decay_rate.reshape(groups, group_width, -1),
        ),
    )
    result = result.transpose(1, 0, 2, 3).reshape(streams, channels, length)
    end_state = end_state.transpose(1, 0, 2, 3).reshape(streams, channels, -1)
    return (result, end_state)


def loss_slopes(mixer_outputs, squares, gain, full_width):
    inv_scale = lax.rsqrt(squares / full_width + eps)[..., None]
    normed = mixer_outputs * inv_scale * gain
    change = normed[:, 1] - normed[:, 0]
    clean_slope = -2.0 * change
    pert_slope = 2.0 * change + 2.0 * teacher_weight * (normed[:, 1] - normed[:, 2])
    return (jnp.stack([clean_slope, pert_slope], 1), inv_scale[:, :2])


def out_slopes(mixer_outputs, norm_slope, inv_scale, inner_sum, gain, full_width):
    value = (
        inv_scale * gain * norm_slope
        - mixer_outputs[:, :2] * inv_scale**3 * (inner_sum / full_width)[..., None]
    )
    return value.astype(jnp.bfloat16)


def per_device(
    feat_clean, feat_pert, feat_teacher, short_taps, residues, decay_rate, out_weight, norm_gain
):
    features = jnp.concatenate([feat_clean, feat_pert, feat_teacher], 0)
    prior = passed_along(features[:, -2:, :], "ctx", 1)
    extended = jnp.concatenate([prior, features], 1)
    rows = features.shape[1]
    width = features.shape[2] // 3

    def filtered(lower, upper):
        first_term = short_taps[0, lower:upper] * extended[:, 2:, lower:upper].astype(jnp.float32)
        second_term = short_taps[1, lower:upper] * extended[:, 1 : rows + 1, lower:upper].astype(
            jnp.float32
        )
        third_term = short_taps[2, lower:upper] * extended[:, :rows, lower:upper].astype(
            jnp.float32
        )
        return first_term + second_term + third_term

    query = filtered(0, width).astype(jnp.bfloat16)
    key_part = filtered(width, 2 * width)
    value_part = filtered(2 * width, 3 * width)
    gated = jnp.swapaxes((key_part * value_part).astype(jnp.bfloat16), 1, 2)
    devices = lax.axis_size("ctx")
    share = width // devices
    first = lax.axis_index("ctx") * share
    local_res = lax.dynamic_slice_in_dim(residues, first, share, 0)
    local_rate = lax.dynamic_slice_in_dim(decay_rate, first, share, 0)
    result, unused = modal_conv(
        lax.all_to_all(gated, "ctx", split_axis=1, concat_axis=2, tiled=True), local_res, local_rate
    )
    conv = lax.all_to_all(
        result.astype(jnp.bfloat16), "ctx", split_axis=2, concat_axis=1, tiled=True
    )
    convolved_rows = jnp.swapaxes(conv, 1, 2)
    gated_product = (query.astype(jnp.float32) * convolved_rows.astype(jnp.float32)).astype(
        jnp.bfloat16
    )
    full_width = norm_gain.shape[0]
    mixing_weight = lax.all_gather(out_weight, "dp", axis=1, tiled=True)
    mixer_outputs = jnp.einsum(
        "snc,cd->snd", gated_product, mixing_weight, preferred_element_type=jnp.float32
    )[None]
    squares = jnp.sum(mixer_outputs * mixer_outputs, -1)
    norm_slope, inv_scale = loss_slopes(mixer_outputs, squares, norm_gain, full_width)
    inner_sum = jnp.sum(norm_gain * norm_slope * mixer_outputs[:, :2], -1)
    output_gradient = out_slopes(
        mixer_outputs, norm_slope, inv_scale, inner_sum, norm_gain, full_width
    )
    product_gradient = jnp.einsum(
        "snd,cd->snc", output_gradient[0], mixing_weight, preferred_element_type=jnp.float32
    )
    conv_slope = jnp.swapaxes(
        (product_gradient * query[:2].astype(jnp.float32)).astype(jnp.bfloat16), 1, 2
    )
    query_slope = product_gradient * convolved_rows[:2].astype(jnp.float32)
    result, unused = modal_conv(
        jnp.flip(lax.all_to_all(conv_slope, "ctx", split_axis=1, concat_axis=2, tiled=True), 2),
        local_res,
        local_rate,
    )
    gated_slope = lax.all_to_all(
        jnp.flip(result, 2).astype(jnp.bfloat16), "ctx", split_axis=2, concat_axis=1, tiled=True
    )
    gated_rows = jnp.swapaxes(gated_slope, 1, 2).astype(jnp.float32)
    unit_slope = jnp.concatenate(
        [query_slope, gated_rows * value_part[:2], gated_rows * key_part[:2]], -1
    )
    after = passed_along(unit_slope[:, :2].astype(jnp.bfloat16), "ctx", -1).astype(jnp.float32)
    extended_slope = jnp.concatenate([unit_slope, after], 1)
    feature_slope = (
        short_taps[0] * extended_slope[:, :-2]
        + short_taps[1] * extended_slope[:, 1:-1]
        + short_taps[2] * extended_slope[:, 2:]
    )
    gradient = feature_slope.astype(jnp.bfloat16)
    return (gradient[0:1], gradient[1:2])


def solution(mesh):
    in_specs = (
        P("dp", "ctx", None),
        P("dp", "ctx", None),
        P("dp", "ctx", None),
        P(),
        P(),
        P(),
        P(None, "dp"),
        P(),
    )
    out_specs = (P("dp", "ctx", None), P("dp", "ctx", None))
    return jax.shard_map(
        per_device, mesh=mesh, in_specs=in_specs, out_specs=out_specs, check_vma=False
    )
```

profile of v0, /device:TPU:0, one launch (start us, length us, event | category | flops | bytes accessed | tf_op | source)
XLA Modules:
  0.0 823.1 jit_solution(247839465695638709)
XLA Ops:
  9.6 4.8 collective-permute-start
  14.6 1.9 collective-permute-done
  16.5 2.4 fusion.150
  18.9 1.4 copy.92
  20.3 2.4 reshape.430
  22.7 6.7 all-to-all-start
  30.4 18.1 %all-to-all-done = bf16[8,2,24576]{2,1,0:T(2,128)(2,1)S(1)} async-done(((bf16[8,2,24576]{2,1,0:T(2,128)(2,1)}), bf16[8,2,24576]{2,1,0:T(2,128)(2,1)S(1)}, u32[]{:S(2)}, u32[]{:S(2)}) %all-to-all-start) | async-done | bytes 786464 | tf_op jit(solution)/shard_map/all_to_all | solution.py:135
  49.8 2.5 copy.166
  52.2 3.5 reshape.378
  55.7 328.3 %while.24 = (s32[]{:T(128)}, bf16[4,3,64,512]{3,2,0,1:T(8,128)(2,1)}, bf16[4,3,64,512]{3,2,0,1:T(8,128)(2,1)}, f32[4,64,16]{2,1,0:T(8,128)S(1)}, f32[4,64,16]{2,1,0:T(8,128)S(1)}, /*index=5*/s32[]{:T(128)}) while((s32[]{:T(128)}, bf16[4,3,64,512]{3,2,0,1:T(8,128)(2,1)}, bf16[4,3,64,512]{3,2,0,1:T(8,128)(2,1)}, f32[4,64,16]{2,1,0:T(8,128)S(1)}, ...), condition=%wide.region_1.3_spmd, body=%wide.region_0.2_spmd.sunk | while | flops 87947616 | bytes 46853440 | solution.py:76
  56.7 54.5 %gather_fusion = f32[16384,64]{1,0:T(8,128)} fusion(f32[64,128]{0,1:T(8,128)S(1)} %bitcast.304, s32[16384]{0:T(1024)S(1)} %bitcast_clamp_fusion.4), kind=kCustom, calls=%fused_computation.clone.clone.1 | custom fusion | bytes 8454144 | tf_op jit(solution)/shard_map/while/body/eval_jaxpr/jit(_take)/gather | solution.py:42
  111.2 7.4 copy.192
  119.7 3.5 fusion.236
  126.6 7.5 fusion.240
  134.2 2.9 fusion.242
  138.7 54.5 %gather_fusion = f32[16384,64]{1,0:T(8,128)} fusion(f32[64,128]{0,1:T(8,128)S(1)} %bitcast.304, s32[16384]{0:T(1024)S(1)} %bitcast_clamp_fusion.4), kind=kCustom, calls=%fused_computation.clone.clone.1 | custom fusion | bytes 8454144 | tf_op jit(solution)/shard_map/while/body/eval_jaxpr/jit(_take)/gather | solution.py:42
  193.2 7.4 copy.192
  201.7 3.5 fusion.236
  208.6 7.5 fusion.240
  216.2 2.9 fusion.242
  220.8 54.5 %gather_fusion = f32[16384,64]{1,0:T(8,128)} fusion(f32[64,128]{0,1:T(8,128)S(1)} %bitcast.304, s32[16384]{0:T(1024)S(1)} %bitcast_clamp_fusion.4), kind=kCustom, calls=%fused_computation.clone.clone.1 | custom fusion | bytes 8454144 | tf_op jit(solution)/shard_map/while/body/eval_jaxpr/jit(_take)/gather | solution.py:42
  275.3 7.4 copy.192
  283.7 3.5 fusion.236
  290.7 7.5 fusion.240
  298.2 2.9 fusion.242
  302.8 54.5 %gather_fusion = f32[16384,64]{1,0:T(8,128)} fusion(f32[64,128]{0,1:T(8,128)S(1)} %bitcast.304, s32[16384]{0:T(1024)S(1)} %bitcast_clamp_fusion.4), kind=kCustom, calls=%fused_computation.clone.clone.1 | custom fusion | bytes 8454144 | tf_op jit(solution)/shard_map/while/body/eval_jaxpr/jit(_take)/gather | solution.py:42
  357.3 7.4 copy.192
  365.7 3.5 fusion.236
  372.7 7.5 fusion.240
  380.3 2.9 fusion.242
  384.0 2.5 copy.98
  386.5 4.4 all-to-all-start.1
  390.9 1.5 add_convert_fusion
  392.4 23.7 %all-to-all-done.1 = bf16[3,256,512]{1,0,2:T(4,128)(2,1)} async-done(((bf16[3,256,512]{1,0,2:T(4,128)(2,1)}), bf16[3,256,512]{1,0,2:T(4,128)(2,1)}, u32[]{:S(2)}, u32[]{:S(2)}) %all-to-all-start.1) | async-done | bytes 786464 | tf_op jit(solution)/shard_map/all_to_all | solution.py:137
  418.4 8.1 multiply_reduce_fusion
  428.7 13.5 %convert_multiply_fusion = (f32[2,64,2048]{2,1,0:T(8,128)}, bf16[2,2048,64]{1,2,0:T(8,128)(2,1)}) fusion(bf16[3,64,2048]{2,1,0:T(8,128)(2,1)} %bitcast.320, bf16[3,64,2048]{2,1,0:T(8,128)(2,1)} %add_convert_fusion, bf16[2048,4096]{1,0:T(8,128)(2,1)} %all-gather.2.cloned.1.call-done, f32[2,64]{1,0:T(2,128)S(1)} %broadcast_multiply_fusion.3, ...), kind=kOutput, calls=%fused_computation.194 | convolution fusion | flops 2152464384 | bytes 23612416 | tf_op jit(solution)/shard_map/snd,cd->snc/dot_general | solution.py:155
  442.2 2.3 copy.101
  444.6 1.5 reshape.432
  446.1 3.7 all-to-all-start.2
  449.8 14.5 %all-to-all-done.2 = bf16[8,2,16384]{2,1,0:T(2,128)(2,1)S(1)} async-done(((bf16[8,2,16384]{2,1,0:T(2,128)(2,1)}), bf16[8,2,16384]{2,1,0:T(2,128)(2,1)S(1)}, u32[]{:S(2)}, u32[]{:S(2)}) %all-to-all-start.2) | async-done | bytes 524320 | tf_op jit(solution)/shard_map/all_to_all | solution.py:163
  466.6 316.8 %while.25 = (s32[]{:T(128)}, bf16[4,2,64,512]{3,2,0,1:T(8,128)(2,1)S(1)}, bf16[4,2,64,512]{3,2,0,1:T(8,128)(2,1)S(1)}, f32[4,64,16]{2,1,0:T(8,128)S(1)}, f32[4,64,16]{2,1,0:T(8,128)S(1)}, /*index=5*/s32[]{:T(128)}) while((s32[]{:T(128)}, bf16[4,2,64,512]{3,2,0,1:T(8,128)(2,1)S(1)}, bf16[4,2,64,512]{3,2,0,1:T(8,128)(2,1)S(1)}, ...), condition=%wide.region_5.7_spmd, body=%wide.region_4.6_spmd.sunk | while | flops 62482788 | bytes 45345604 | solution.py:76
  468.6 7.5 fusion.259
  476.1 2.1 fusion.261
  479.1 54.5 %gather_fusion.1 = f32[16384,64]{1,0:T(8,128)} fusion(f32[64,128]{0,1:T(8,128)S(1)} %bitcast.305, s32[16384]{0:T(1024)S(1)} %bitcast_clamp_fusion.5), kind=kCustom, calls=%fused_computation.1.clone.clone.1 | custom fusion | bytes 8454144 | tf_op jit(solution)/shard_map/while/body/eval_jaxpr/jit(_take)/gather | solution.py:42
  533.5 7.4 copy.202
  541.0 3.5 fusion.264
  547.8 7.5 fusion.259
  555.3 2.1 fusion.261
  558.3 54.5 %gather_fusion.1 = f32[16384,64]{1,0:T(8,128)} fusion(f32[64,128]{0,1:T(8,128)S(1)} %bitcast.305, s32[16384]{0:T(1024)S(1)} %bitcast_clamp_fusion.5), kind=kCustom, calls=%fused_computation.1.clone.clone.1 | custom fusion | bytes 8454144 | tf_op jit(solution)/shard_map/while/body/eval_jaxpr/jit(_take)/gather | solution.py:42
  612.7 7.4 copy.202
  620.2 3.5 fusion.264
  627.0 7.5 fusion.259
  634.5 2.1 fusion.261
  637.5 54.5 %gather_fusion.1 = f32[16384,64]{1,0:T(8,128)} fusion(f32[64,128]{0,1:T(8,128)S(1)} %bitcast.305, s32[16384]{0:T(1024)S(1)} %bitcast_clamp_fusion.5), kind=kCustom, calls=%fused_computation.1.clone.clone.1 | custom fusion | bytes 8454144 | tf_op jit(solution)/shard_map/while/body/eval_jaxpr/jit(_take)/gather | solution.py:42
  691.9 7.4 copy.202
  699.4 3.5 fusion.264
  706.2 7.5 fusion.259
  713.7 2.1 fusion.261
  716.7 54.5 %gather_fusion.1 = f32[16384,64]{1,0:T(8,128)} fusion(f32[64,128]{0,1:T(8,128)S(1)} %bitcast.305, s32[16384]{0:T(1024)S(1)} %bitcast_clamp_fusion.5), kind=kCustom, calls=%fused_computation.1.clone.clone.1 | custom fusion | bytes 8454144 | tf_op jit(solution)/shard_map/while/body/eval_jaxpr/jit(_take)/gather | solution.py:42
  771.1 7.4 copy.202
  778.6 3.5 fusion.264
  783.5 1.7 rev.9
  785.6 18.1 %all_to_all.60 = bf16[2,256,512]{1,0,2:T(2,128)(2,1)S(1)} all-to-all(bf16[2,256,512]{1,0,2:T(2,128)(2,1)S(1)} %copy.107), channel_id=1, replica_groups=mesh['dp'=4,'ctx'=8] {'ctx'}, dimensions={2} | all-to-all | bytes 1048576 | tf_op jit(solution)/shard_map/all_to_all | solution.py:167
  808.5 4.6 collective-permute-done.1
  (241 shorter events, 59.7 us)
Async XLA Ops:
  7.2 1.1 copy-start.9
  7.2 1.4 copy-start.10
  7.2 411.3 %all-gather.2.cloned.1.call-start = ((), (), s32[]{:S(2)}) async-start(), calls=%async_computation.4 | async-start | bytes 20971520 | tf_op jit(solution)/shard_map/all_gather | solution.py:145
  8.3 1.2 copy-start.11
  8.3 6.2 copy-start.13
  9.5 9.4 %copy-start.2 = (bf16[3,64,6144]{2,1,0:T(8,128)(2,1)}, bf16[3,64,6144]{2,1,0:T(8,128)(2,1)S(1)}, u32[]{:S(2)}) copy-start(bf16[3,64,6144]{2,1,0:T(8,128)(2,1)S(1)} %constant_dynamic-update-slice_fusion) | copy-start | bytes 7077892
  9.6 6.8 collective-permute-start
  22.7 25.8 %all-to-all-start = ((bf16[8,2,24576]{2,1,0:T(2,128)(2,1)}), bf16[8,2,24576]{2,1,0:T(2,128)(2,1)S(1)}, u32[]{:S(2)}, u32[]{:S(2)}) async-start(bf16[8,2,24576]{2,1,0:T(2,128)(2,1)} %reshape.430), calls=%async_computation | async-start | bytes 1572864 | tf_op jit(solution)/shard_map/all_to_all | solution.py:135
  119.6 3.5 copy-start
  201.7 3.5 copy-start
  283.7 3.5 copy-start
  365.7 3.5 copy-start
  384.0 6.9 copy-start.3
  386.5 29.6 %all-to-all-start.1 = ((bf16[3,256,512]{1,0,2:T(4,128)(2,1)}), bf16[3,256,512]{1,0,2:T(4,128)(2,1)}, u32[]{:S(2)}, u32[]{:S(2)}) async-start(bf16[3,256,512]{1,0,2:T(4,128)(2,1)} %copy.98), calls=%async_computation.1 | async-start | bytes 2097152 | tf_op jit(solution)/shard_map/all_to_all | solution.py:137
  418.4 8.2 copy-start.12
  427.4 1.0 copy-start.5
  427.4 1.3 copy-start.6
  446.1 18.3 %all-to-all-start.2 = ((bf16[8,2,16384]{2,1,0:T(2,128)(2,1)}), bf16[8,2,16384]{2,1,0:T(2,128)(2,1)S(1)}, u32[]{:S(2)}, u32[]{:S(2)}) async-start(bf16[8,2,16384]{2,1,0:T(2,128)(2,1)} %reshape.432), calls=%async_computation.2 | async-start | bytes 1048576 | tf_op jit(solution)/shard_map/all_to_all | solution.py:163
  541.0 3.5 copy-start.1
  620.2 3.5 copy-start.1
  699.4 3.5 copy-start.1
  778.6 3.5 copy-start.1
  803.8 1.4 copy-start.7
  803.8 1.9 copy-start.8
  805.7 1.2 copy-start.4
  806.9 1.5 copy-start.14
  807.1 6.0 collective-permute-start.1
Sparse Core Ops, SparseCore 0:
  9.6 108.6 all-gather.1
where the time goes:
time: 828 us; the launch traced here: 823 us
  local copies, waits for them, and re-layouts  545 us (66%)
  matrix products  151 us (18%)
  waiting for transfers between devices  63.6 us (8%)
  starting transfers between devices  21.1 us (3%)
  blocking collectives  18.1 us (2%)
  between operations  14.8 us (2%)
  other arithmetic  9.11 us (1%)
    gather x16, local copies, waits for them, and re-layouts, modal_group(): jnp.take(kernel, jnp.clip(offset, 0, block - 1), axis=1)  495 us
    dot_general x8, matrix products, modal_group(): jnp.einsum('gmab,sgbm->sgam', carry_map, block_ends, precision=highest)  60.2 us
    dot_general x16, matrix products, split_product(): jnp.einsum(form, lower, data, preferred_element_type=jnp.float32)  30.9 us
    all_to_all x1, waiting for transfers between devices, per_device(): lax.all_to_all(result.astype(jnp.bfloat16), 'ctx', split_axis=2, concat_a...  23.7 us
    dot_general x8, matrix products, modal_group(): between = jnp.einsum('gmi,sgkm->sgki', reach_map, states, precision=highest)  20.1 us
    all_to_all x1, waiting for transfers between devices, per_device(): lax.all_to_all(gated, 'ctx', split_axis=1, concat_axis=2, tiled=True)  18.1 us
    all_to_all x1, blocking collectives, per_device(): lax.all_to_all(jnp.flip(result, 2).astype(jnp.bfloat16), 'ctx', split_axi...  18.1 us
  transfers between devices with their start and end apart: 6, of which 5 were waited for; matrix products, arithmetic and copies ran while one was open for 42% of the time, Pallas kernels for 0%

commit v1 on v0

v1 whole, which is shorter than its diff:
```python
import math

import jax
import jax.numpy as jnp
from jax import lax
from jax.experimental import pallas as pl
from jax.experimental.pallas import tpu as pltpu
from jax.sharding import PartitionSpec as P

eps = 1e-06
teacher_weight = 0.5
f32 = jnp.float32
bf16 = jnp.bfloat16
LANES = 128
SUB = 8


def row_index():
    return lax.broadcasted_iota(jnp.int32, (SUB, LANES), 0).astype(f32)


def split_rows(value):
    return [value[SUB * i : SUB * (i + 1)] for i in range(value.shape[0] // SUB)]


def shifted_down(value, steps):
    if steps == 0:
        return value
    rows = lax.broadcasted_iota(jnp.int32, value.shape, 0)
    return jnp.where(rows >= steps, pltpu.roll(value, steps, 0), 0.0)


def shifted_up(value, steps):
    if steps == 0:
        return value
    count = value.shape[0]
    rows = lax.broadcasted_iota(jnp.int32, value.shape, 0)
    return jnp.where(rows < count - steps, pltpu.roll(value, count - steps, 0), 0.0)


def filter_table(res, rate, rows):
    row = row_index()
    tiles = [jnp.zeros((SUB, LANES), f32) for _ in range(rows // SUB)]
    for m in range(res.shape[0]):
        current = res[m : m + 1] * jnp.exp(-rate[m : m + 1] * row)
        step = jnp.exp(-rate[m : m + 1] * SUB)
        for i in range(len(tiles)):
            tiles[i] = tiles[i] + current
            current = current * step
    return jnp.concatenate(tiles, 0)


def direct_conv(value, table_row, causal):
    count = value.shape[0] // SUB
    out = [jnp.zeros((SUB, LANES), f32) for _ in range(count)]
    for b in range(SUB):
        tiles = split_rows(shifted_down(value, b) if causal else shifted_up(value, b))
        for a in range(count):
            weight = jnp.broadcast_to(table_row(SUB * a + b), (SUB, LANES))
            for i in range(count - a):
                if causal:
                    out[i + a] = out[i + a] + weight * tiles[i]
                else:
                    out[i] = out[i] + weight * tiles[i + a]
    return jnp.concatenate(out, 0)


def block_states(values, rate, causal, store):
    row = row_index()
    split = [split_rows(value) for value in values]
    count = len(split[0])
    for m in range(rate.shape[0]):
        one = rate[m : m + 1]
        step = jnp.exp(-one * SUB)
        if causal:
            current, order = jnp.exp(-one * (SUB - 1.0 - row)), range(count - 1, -1, -1)
        else:
            current, order = jnp.exp(-one * row), range(count)
        sums = [jnp.zeros((SUB, LANES), f32) for _ in split]
        for place, i in enumerate(order):
            sums = [total + current * tiles[i] for total, tiles in zip(sums, split)]
            if place < count - 1:
                current = current * step
        for s, total in enumerate(sums):
            store(s, m, jnp.sum(total, 0, keepdims=True))


def reached(locals_, state_row, res, rate, causal):
    row = row_index()
    split = [split_rows(value) for value in locals_]
    count = len(split[0])
    for m in range(rate.shape[0]):
        one = rate[m : m + 1]
        step = jnp.exp(-one * SUB)
        if causal:
            current, order = res[m : m + 1] * jnp.exp(-one * (row + 1.0)), range(count)
        else:
            current, order = res[m : m + 1] * jnp.exp(-one * (SUB - row)), range(count - 1, -1, -1)
        states = [jnp.broadcast_to(state_row(s, m), (SUB, LANES)) for s in range(len(split))]
        for place, i in enumerate(order):
            for s, tiles in enumerate(split):
                tiles[i] = tiles[i] + current * states[s]
            if place < count - 1:
                current = current * step
    return [jnp.concatenate(tiles, 0) for tiles in split]


def lane_loop(width, body):
    def step(i, carry):
        body(pl.ds(pl.multiple_of(i * LANES, LANES), LANES))
        return carry

    lax.fori_loop(0, width // LANES, step, 0)


def dp_peers():
    me = lax.axis_index("dp")
    chip, core = me // 2, me % 2
    sibling = chip * 2 + (1 - core)
    across = (1 - chip) * 2 + core
    diagonal = (1 - chip) * 2 + (1 - core)
    return me, sibling, across, diagonal


def mixer_kernel(
    prod_ref,
    weight_ref,
    gain_ref,
    slope_ref,
    rows_ref,
    y_ref,
    tile_ref,
    sums_ref,
    out_ref,
    hold_ref,
    send_ref,
    land_ref,
    send_sem,
    recv_sem,
    sum_send,
    sum_recv,
    back_send,
    back_recv,
):
    _, rows, width = prod_ref.shape
    own_width = weight_ref.shape[1]
    full_width = own_width * lax.axis_size("dp")
    me, sibling, across, diagonal = dp_peers()

    barrier = pltpu.get_barrier_semaphore()
    for peer in (sibling, across, diagonal):
        pl.semaphore_signal(
            barrier, inc=1, device_id={"dp": peer}, device_id_type=pl.DeviceIdType.MESH
        )
    pl.semaphore_wait(barrier, 3)

    def copy(source, target, send, recv, peer):
        return pltpu.make_async_remote_copy(
            src_ref=source,
            dst_ref=target,
            send_sem=send,
            recv_sem=recv,
            device_id={"dp": peer},
            device_id_type=pl.DeviceIdType.MESH,
        )

    forward = {}
    for s in range(3):
        for slot, peer in ((1, across), (0, sibling)):
            span = pl.ds(s * rows, rows)
            forward[slot, s] = copy(
                prod_ref.at[s],
                rows_ref.at[slot, span],
                send_sem.at[slot, s],
                recv_sem.at[slot, s],
                peer,
            )
            forward[slot, s].start()

    tile = min(256, own_width)

    def project(source, place):
        def step(i, carry):
            lanes = pl.ds(pl.multiple_of(i * tile, tile), tile)
            y_ref[place, :, lanes] = jnp.dot(
                source(), weight_ref[:, lanes], preferred_element_type=f32
            )
            return carry

        lax.fori_loop(0, own_width // tile, step, 0)

    def add_up(place):
        lane = lax.broadcasted_iota(jnp.int32, (SUB, LANES), 1)

        def step(i, carry):
            first = pl.multiple_of(i * SUB, SUB)
            yc, yp, yt = [y_ref[place, pl.ds(first + s * rows, SUB), :] for s in range(3)]
            gc, gp, gt = [gain_ref[...] * y for y in (yc, yp, yt)]
            pairs = ((yc, yc), (yp, yp), (yt, yt), (gc, gc), (gp, gp), (gc, gp), (gp, gt))
            result = jnp.zeros((SUB, LANES), f32)
            for n, (a, b) in enumerate(pairs):
                result = jnp.where(lane == n, jnp.sum(a * b, 1, keepdims=True), result)
            tile_ref[pl.ds(pl.multiple_of(place * rows + first, SUB), SUB), :] = result
            return carry

        lax.fori_loop(0, rows // SUB, step, 0)

    project(lambda: prod_ref[...].reshape(3 * rows, width), 0)
    add_up(0)
    for s in range(3):
        forward[1, s].wait_recv()
        span = pl.ds(s * rows, rows)
        forward[2, s] = copy(
            rows_ref.at[1, span],
            rows_ref.at[2, span],
            send_sem.at[2, s],
            recv_sem.at[2, s],
            sibling,
        )
        forward[2, s].start()
    for s in range(3):
        forward[0, s].wait_recv()
    project(lambda: rows_ref[0], 1)
    add_up(1)
    project(lambda: rows_ref[1], 2)
    add_up(2)
    for s in range(3):
        forward[2, s].wait_recv()
    project(lambda: rows_ref[2], 3)
    add_up(3)
    for s in range(3):
        for slot in range(3):
            forward[slot, s].wait_send()

    packed = tile_ref[...].T[:SUB]
    owners = (me, sibling, across, diagonal)
    for place, owner in enumerate(owners):
        sums_ref[me, owner] = packed[:, place * rows : (place + 1) * rows]
    exchanged = [
        copy(sums_ref.at[me], sums_ref.at[me], sum_send.at[n], sum_recv.at[n], peer)
        for n, peer in enumerate((sibling, across, diagonal))
    ]
    for one in exchanged:
        one.start()
    for one in exchanged:
        one.wait()
    total = sums_ref[0] + sums_ref[1] + sums_ref[2] + sums_ref[3]
    sums_ref[me] = total
    for place, owner in enumerate(owners):
        columns = jnp.concatenate(
            [sums_ref[me, owner], jnp.zeros((LANES - SUB, rows), f32)], 0
        )
        tile_ref[place * rows : (place + 1) * rows, :] = columns.T

    def slopes(place):
        high = 16

        def step(i, carry):
            first = pl.multiple_of(i * high, high)
            yc, yp, yt = [y_ref[place, pl.ds(first + s * rows, high), :] for s in range(3)]
            sums = tile_ref[pl.ds(pl.multiple_of(place * rows + first, high), high), :]
            inv_c, inv_p, inv_t = [
                lax.rsqrt(sums[:, n : n + 1] / full_width + eps) for n in range(3)
            ]
            cc, pp, cp, pt = [sums[:, n : n + 1] for n in range(3, 7)]
            inner_c = -2.0 * (inv_p * cp - inv_c * cc)
            inner_p = 2.0 * (inv_p * pp - inv_c * cp) + 2.0 * teacher_weight * (
                inv_p * pp - inv_t * pt
            )
            gain = gain_ref[...]
            nc, np_, nt = yc * inv_c * gain, yp * inv_p * gain, yt * inv_t * gain
            change = np_ - nc
            slope_c = -2.0 * change
            slope_p = 2.0 * change + 2.0 * teacher_weight * (np_ - nt)
            out_c = inv_c * gain * slope_c - yc * (inv_c * inv_c * inv_c * (inner_c / full_width))
            out_p = inv_p * gain * slope_p - yp * (inv_p * inv_p * inv_p * (inner_p / full_width))
            out_ref[place, pl.ds(first, high), :] = out_c.astype(bf16)
            out_ref[place, pl.ds(pl.multiple_of(rows + first, high), high), :] = out_p.astype(bf16)
            return carry

        lax.fori_loop(0, rows // high, step, 0)

    wide = min(256, width)

    def pull(place, store):
        def step(i, carry):
            lanes = pl.ds(pl.multiple_of(i * wide, wide), wide)
            store(
                lanes,
                lax.dot_general(
                    out_ref[place],
                    weight_ref[lanes, :],
                    (((1,), (1,)), ((), ())),
                    preferred_element_type=f32,
                ),
            )
            return carry

        lax.fori_loop(0, width // wide, step, 0)

    def to_send(slot):
        def store(lanes, value):
            send_ref[slot, :, lanes] = value.astype(bf16)

        return store

    def to_hold(lanes, value):
        hold_ref[:, lanes] = value

    backward = [
        copy(send_ref.at[n], land_ref.at[n], back_send.at[n], back_recv.at[n], peer)
        for n, peer in enumerate((sibling, across, sibling))
    ]
    slopes(3)
    pull(3, to_send(0))
    backward[0].start()
    slopes(2)
    pull(2, to_hold)
    backward[0].wait_recv()

    def join(i, carry):
        lanes = pl.ds(pl.multiple_of(i * wide, wide), wide)
        send_ref[1, :, lanes] = (hold_ref[:, lanes] + land_ref[0, :, lanes].astype(f32)).astype(bf16)
        return carry

    lax.fori_loop(0, width // wide, join, 0)
    backward[1].start()
    slopes(1)
    pull(1, to_send(2))
    backward[2].start()
    slopes(0)
    pull(0, to_hold)
    backward[2].wait_recv()
    backward[1].wait_recv()

    def finish(i, carry):
        lanes = pl.ds(pl.multiple_of(i * wide, wide), wide)
        total = (
            hold_ref[:, lanes]
            + land_ref[2, :, lanes].astype(f32)
            + land_ref[1, :, lanes].astype(f32)
        )
        slope_ref[0, :, lanes] = total[:rows]
        slope_ref[1, :, lanes] = total[rows:]
        return carry

    lax.fori_loop(0, width // wide, finish, 0)
    for one in backward:
        one.wait_send()


def mixer(prod, weight, gain):
    _, rows, width = prod.shape
    own_width = weight.shape[1]
    return pl.pallas_call(
        mixer_kernel,
        in_specs=[pl.BlockSpec(memory_space=pltpu.VMEM)] * 3,
        out_specs=pl.BlockSpec(memory_space=pltpu.VMEM),
        out_shape=jax.ShapeDtypeStruct((2, rows, width), f32),
        scratch_shapes=[
            pltpu.VMEM((3, 3 * rows, width), bf16),
            pltpu.VMEM((4, 3 * rows, own_width), f32),
            pltpu.VMEM((4 * rows, LANES), f32),
            pltpu.VMEM((4, 4, SUB, rows), f32),
            pltpu.VMEM((4, 2 * rows, own_width), bf16),
            pltpu.VMEM((2 * rows, width), f32),
            pltpu.VMEM((3, 2 * rows, width), bf16),
            pltpu.VMEM((3, 2 * rows, width), bf16),
            pltpu.SemaphoreType.DMA((3, 3)),
            pltpu.SemaphoreType.DMA((3, 3)),
            pltpu.SemaphoreType.DMA((3,)),
            pltpu.SemaphoreType.DMA((3,)),
            pltpu.SemaphoreType.DMA((3,)),
            pltpu.SemaphoreType.DMA((3,)),
        ],
        compiler_params=pltpu.CompilerParams(
            collective_id=0, has_side_effects=True, vmem_limit_bytes=56 * 2**20
        ),
        name="mixer",
    )(prod, weight, gain)


def ctx_line():
    me = lax.axis_index("ctx")
    count = lax.axis_size("ctx")
    return me, count, lax.rem(me + 1, count), lax.rem(me + count - 1, count)


def greet(peers):
    barrier = pltpu.get_barrier_semaphore()
    for peer in peers:
        pl.semaphore_signal(
            barrier, inc=1, device_id={"ctx": peer}, device_id_type=pl.DeviceIdType.MESH
        )
    pl.semaphore_wait(barrier, len(peers))


def ctx_copy(source, target, send, recv, peer):
    return pltpu.make_async_remote_copy(
        src_ref=source,
        dst_ref=target,
        send_sem=send,
        recv_sem=recv,
        device_id={"ctx": peer},
        device_id_type=pl.DeviceIdType.MESH,
    )


def carry_states(going_ref, coming_ref, rate_ref, rows, send_sem, recv_sem, peer, is_first, is_last):
    pieces = send_sem.shape[0]
    modes, width = rate_ref.shape
    streams = going_ref.shape[0]
    piece = width // pieces
    copies = [
        ctx_copy(
            going_ref.at[:, :, pl.ds(c * piece, piece)],
            coming_ref.at[:, :, pl.ds(c * piece, piece)],
            send_sem.at[c],
            recv_sem.at[c],
            peer,
        )
        for c in range(pieces)
    ]

    @pl.when(is_first)
    def _():
        coming_ref[...] = jnp.zeros(coming_ref.shape, f32)

    for c in range(pieces):

        @pl.when(jnp.logical_not(is_first))
        def _():
            copies[c].wait_recv()

        @pl.when(jnp.logical_not(is_last))
        def _():
            def step(i, carry):
                lanes = pl.ds(pl.multiple_of(c * piece + i * LANES, LANES), LANES)
                decay = jnp.exp(-rate_ref[:, lanes] * rows)
                for s in range(streams):
                    going_ref[s, :, lanes] = going_ref[s, :, lanes] + decay * coming_ref[s, :, lanes]
                return carry

            lax.fori_loop(0, piece // LANES, step, 0)
            copies[c].start()

    def settle():
        @pl.when(jnp.logical_not(is_last))
        def _():
            for one in copies:
                one.wait_send()

    return settle


def front_kernel(
    clean_ref,
    pert_ref,
    teacher_ref,
    tap_ref,
    res_ref,
    rate_ref,
    query_ref,
    key_ref,
    value_ref,
    conv_ref,
    prod_ref,
    table_ref,
    halo_out,
    halo_in,
    gated_ref,
    going_ref,
    coming_ref,
    halo_sem,
    send_sem,
    recv_sem,
):
    feats = (clean_ref, pert_ref, teacher_ref)
    rows, width = clean_ref.shape[1], clean_ref.shape[2] // 3
    me, count, after, before = ctx_line()
    is_first, is_last = me == 0, me == count - 1
    greet((after, before))

    def heads(lanes):
        tails = [f[0, rows - 16 :, lanes].astype(f32)[14:] for f in feats]
        halo_out[:, lanes] = jnp.concatenate(tails + [jnp.zeros((2, LANES), f32)], 0)

    lane_loop(3 * width, heads)
    halo = ctx_copy(halo_out, halo_in, halo_sem.at[0], halo_sem.at[1], after)

    @pl.when(jnp.logical_not(is_last))
    def _():
        halo.start()

    def tables(lanes):
        table_ref[:, lanes] = filter_table(res_ref[:, lanes], rate_ref[:, lanes], rows)

    lane_loop(width, tables)

    @pl.when(is_first)
    def _():
        halo_in[...] = jnp.zeros(halo_in.shape, f32)

    @pl.when(jnp.logical_not(is_first))
    def _():
        halo.wait_recv()

    row = lambda: lax.broadcasted_iota(jnp.int32, (rows, LANES), 0)

    def filtered(s, lanes):
        here = feats[s][0, :, lanes].astype(f32)
        back_two, back_one = halo_in[2 * s : 2 * s + 1, lanes], halo_in[2 * s + 1 : 2 * s + 2, lanes]
        one = jnp.where(row() >= 1, pltpu.roll(here, 1, 0), back_one)
        two = jnp.where(
            row() >= 2, pltpu.roll(here, 2, 0), jnp.where(row() == 1, back_one, back_two)
        )
        return (
            tap_ref[0:1, lanes] * here + tap_ref[1:2, lanes] * one + tap_ref[2:3, lanes] * two
        )

    def features(i, carry):
        lanes, klanes, vlanes = [
            pl.ds(pl.multiple_of(i * LANES + j * width, LANES), LANES) for j in range(3)
        ]
        gated = []
        for s in range(3):
            query_ref[s, :, lanes] = filtered(s, lanes).astype(bf16)
            k, v = filtered(s, klanes), filtered(s, vlanes)
            if s < 2:
                key_ref[s, :, lanes] = k
                value_ref[s, :, lanes] = v
            gated.append((k * v).astype(bf16).astype(f32))
            gated_ref[s, :, lanes] = gated[s]

        def store(s, m, value):
            going_ref[s, pl.ds(m, 1), lanes] = value

        block_states(gated, rate_ref[:, lanes], True, store)
        return carry

    lax.fori_loop(0, width // LANES, features, 0)

    def direct(lanes):
        for s in range(3):
            gated_ref[s, :, lanes] = direct_conv(
                gated_ref[s, :, lanes], lambda j: table_ref[pl.ds(j, 1), lanes], True
            )

    late = me >= count // 2

    @pl.when(late)
    def _():
        lane_loop(width, direct)

    settle = carry_states(
        going_ref, coming_ref, rate_ref, rows, send_sem, recv_sem, after, is_first, is_last
    )

    @pl.when(jnp.logical_not(late))
    def _():
        lane_loop(width, direct)

    def finish(lanes):
        full = reached(
            [gated_ref[s, :, lanes] for s in range(3)],
            lambda s, m: coming_ref[s, pl.ds(m, 1), lanes],
            res_ref[:, lanes],
            rate_ref[:, lanes],
            True,
        )
        for s in range(3):
            conv = full[s].astype(bf16)
            if s < 2:
                conv_ref[s, :, lanes] = conv
            prod_ref[s, :, lanes] = (
                query_ref[s, :, lanes].astype(f32) * conv.astype(f32)
            ).astype(bf16)

    lane_loop(width, finish)
    settle()

    @pl.when(jnp.logical_not(is_last))
    def _():
        halo.wait_send()


def pieces_of(width):
    return math.gcd(width // LANES, 4)


def front(feats, taps, res, rate):
    _, rows, width3 = feats[0].shape
    width, modes = width3 // 3, res.shape[0]
    pieces = pieces_of(width)
    vmem = pl.BlockSpec(memory_space=pltpu.VMEM)
    return pl.pallas_call(
        front_kernel,
        in_specs=[vmem] * 6,
        out_specs=[vmem] * 6,
        out_shape=[
            jax.ShapeDtypeStruct((3, rows, width), bf16),
            jax.ShapeDtypeStruct((2, rows, width), f32),
            jax.ShapeDtypeStruct((2, rows, width), f32),
            jax.ShapeDtypeStruct((2, rows, width), bf16),
            jax.ShapeDtypeStruct((3, rows, width), bf16),
            jax.ShapeDtypeStruct((rows, width), f32),
        ],
        scratch_shapes=[
            pltpu.VMEM((SUB, 3 * width), f32),
            pltpu.VMEM((SUB, 3 * width), f32),
            pltpu.VMEM((3, rows, width), f32),
            pltpu.VMEM((3, modes, width), f32),
            pltpu.VMEM((3, modes, width), f32),
            pltpu.SemaphoreType.DMA((2,)),
            pltpu.SemaphoreType.DMA((pieces,)),
            pltpu.SemaphoreType.DMA((pieces,)),
        ],
        compiler_params=pltpu.CompilerParams(
            collective_id=1, has_side_effects=True, vmem_limit_bytes=56 * 2**20
        ),
        name="front",
    )(*feats, taps, res, rate)


def back_kernel(
    slope_ref,
    query_ref,
    key_ref,
    value_ref,
    conv_ref,
    table_ref,
    tap_ref,
    res_ref,
    rate_ref,
    clean_ref,
    pert_ref,
    halo_out,
    halo_in,
    local_ref,
    tail_ref,
    going_ref,
    coming_ref,
    halo_sem,
    send_sem,
    recv_sem,
):
    grads = (clean_ref, pert_ref)
    _, rows, width = slope_ref.shape
    me, count, after, before = ctx_line()
    is_first, is_last = me == count - 1, me == 0
    greet((after, before))

    def slopes(lanes):
        values = [
            (slope_ref[s, :, lanes] * query_ref[s, :, lanes].astype(f32)).astype(bf16).astype(f32)
            for s in range(2)
        ]
        for s in range(2):
            local_ref[s, :, lanes] = values[s]

        def store(s, m, value):
            going_ref[s, pl.ds(m, 1), lanes] = value

        block_states(values, rate_ref[:, lanes], False, store)

    lane_loop(width, slopes)

    def direct(lanes):
        for s in range(2):
            local_ref[s, :, lanes] = direct_conv(
                local_ref[s, :, lanes], lambda j: table_ref[pl.ds(j, 1), lanes], False
            )

    late = me < count // 2

    @pl.when(late)
    def _():
        lane_loop(width, direct)

    settle = carry_states(
        going_ref, coming_ref, rate_ref, rows, send_sem, recv_sem, before, is_first, is_last
    )

    @pl.when(jnp.logical_not(late))
    def _():
        lane_loop(width, direct)

    def tapped(unit, lanes, next_one, next_two):
        high = unit.shape[0]
        row = lax.broadcasted_iota(jnp.int32, unit.shape, 0)
        one = jnp.where(row < high - 1, pltpu.roll(unit, high - 1, 0), next_one)
        two = jnp.where(
            row < high - 2,
            pltpu.roll(unit, high - 2, 0),
            jnp.where(row == high - 2, next_one, next_two),
        )
        return (
            tap_ref[0:1, lanes] * unit + tap_ref[1:2, lanes] * one + tap_ref[2:3, lanes] * two
        ).astype(bf16)

    def units(i, carry):
        places = [pl.ds(pl.multiple_of(i * LANES + j * width, LANES), LANES) for j in range(3)]
        lanes = places[0]
        full = reached(
            [local_ref[s, :, lanes] for s in range(2)],
            lambda s, m: coming_ref[s, pl.ds(m, 1), lanes],
            res_ref[:, lanes],
            rate_ref[:, lanes],
            False,
        )
        none = jnp.zeros((1, LANES), f32)
        for j, place in enumerate(places):
            firsts = []
            for s in range(2):
                if j == 0:
                    unit = slope_ref[s, :, lanes] * conv_ref[s, :, lanes].astype(f32)
                else:
                    other = value_ref if j == 1 else key_ref
                    unit = full[s].astype(bf16).astype(f32) * other[s, :, lanes]
                firsts.append(unit[:2])
                tail_ref[s, :, place] = unit[rows - 16 :]
                grads[s][0, :, place] = tapped(unit, place, none, none)
            halo_out[:, place] = jnp.concatenate(firsts + [jnp.zeros((4, LANES), f32)], 0)
        return carry

    lax.fori_loop(0, width // LANES, units, 0)
    halo = ctx_copy(halo_out, halo_in, halo_sem.at[0], halo_sem.at[1], before)

    @pl.when(jnp.logical_not(is_last))
    def _():
        halo.start()

    @pl.when(jnp.logical_not(is_first))
    def _():
        halo.wait_recv()

        def mend(lanes):
            for s in range(2):
                grads[s][0, rows - 16 :, lanes] = tapped(
                    tail_ref[s, :, lanes],
                    lanes,
                    halo_in[2 * s : 2 * s + 1, lanes],
                    halo_in[2 * s + 1 : 2 * s + 2, lanes],
                )

        lane_loop(3 * width, mend)

    settle()

    @pl.when(jnp.logical_not(is_last))
    def _():
        halo.wait_send()


def back(prod_slope, query, key_part, value_part, conv, table, taps, res, rate):
    _, rows, width = prod_slope.shape
    modes = res.shape[0]
    pieces = pieces_of(width)
    vmem = pl.BlockSpec(memory_space=pltpu.VMEM)
    return pl.pallas_call(
        back_kernel,
        in_specs=[vmem] * 9,
        out_specs=[vmem] * 2,
        out_shape=[jax.ShapeDtypeStruct((1, rows, 3 * width), bf16)] * 2,
        scratch_shapes=[
            pltpu.VMEM((SUB, 3 * width), f32),
            pltpu.VMEM((SUB, 3 * width), f32),
            pltpu.VMEM((2, rows, width), f32),
            pltpu.VMEM((2, 16, 3 * width), f32),
            pltpu.VMEM((2, modes, width), f32),
            pltpu.VMEM((2, modes, width), f32),
            pltpu.SemaphoreType.DMA((2,)),
            pltpu.SemaphoreType.DMA((pieces,)),
            pltpu.SemaphoreType.DMA((pieces,)),
        ],
        compiler_params=pltpu.CompilerParams(
            collective_id=2, has_side_effects=True, vmem_limit_bytes=56 * 2**20
        ),
        name="back",
    )(prod_slope, query, key_part, value_part, conv, table, taps, res, rate)


def per_device(
    feat_clean, feat_pert, feat_teacher, short_taps, residues, decay_rate, out_weight, norm_gain
):
    res, rate = residues.T, decay_rate.T
    query, key_part, value_part, conv, prod, table = front(
        (feat_clean, feat_pert, feat_teacher), short_taps, res, rate
    )
    own_width = out_weight.shape[1]
    gain = lax.dynamic_slice_in_dim(norm_gain, lax.axis_index("dp") * own_width, own_width, 0)
    prod_slope = mixer(prod, out_weight, gain[None])
    return back(prod_slope, query, key_part, value_part, conv, table, short_taps, res, rate)


def solution(mesh):
    in_specs = (
        P("dp", "ctx", None),
        P("dp", "ctx", None),
        P("dp", "ctx", None),
        P(),
        P(),
        P(),
        P(None, "dp"),
        P(),
    )
    out_specs = (P("dp", "ctx", None), P("dp", "ctx", None))
    return jax.shard_map(
        per_device, mesh=mesh, in_specs=in_specs, out_specs=out_specs, check_vma=False
    )
```

time: 828 us -> 155 us (0.19)
  local copies, waits for them, and re-layouts: 545 us -> 5.41 us
  matrix products: 151 us -> 0 us
  Pallas kernels: 0 us -> 149 us
  waiting for transfers between devices: 63.6 us -> 0 us
  starting transfers between devices: 21.1 us -> 0 us
  blocking collectives: 18.1 us -> 0 us
  between operations: 14.8 us -> 0.66 us
  other arithmetic: 9.11 us -> 0 us
    gather x16 -> x0, local copies, waits for them, and re-layouts: 495 us -> none  [modal_group(): jnp.take(kernel, jnp.clip(offset, 0, block - 1), axis=1)]
    dot_general x58 -> x0, matrix products: 151 us -> none  [the longest x8 60.2 us: modal_group(): jnp.einsum('gmab,sgbm->sgam', carry_map, block_ends, precision=highest)]
    pallas_call x0 -> x3, Pallas kernels: none -> 149 us  [the longest x1 70.2 us: back(): pl.pallas_call(back_kernel, in_specs=[vmem] * 9, out_specs=[vmem] * 2, ou...]
    all_to_all x3 -> x0, waiting for transfers between devices: 56.4 us -> none  [the longest x1 23.7 us: per_device(): lax.all_to_all(result.astype(jnp.bfloat16), 'ctx', split_axis=2, concat_a...]
    all_to_all x1 -> x0, blocking collectives: 18.1 us -> none  [per_device(): lax.all_to_all(jnp.flip(result, 2).astype(jnp.bfloat16), 'ctx', split_axi...]
    all_to_all x3 -> x0, starting transfers between devices: 14.9 us -> none  [the longest x1 6.68 us: per_device(): lax.all_to_all(gated, 'ctx', split_axis=1, concat_axis=2, tiled=True)]
    add x8 -> x0, local copies, waits for them, and re-layouts: 9.25 us -> none  [split_product(): jnp.einsum(form, upper, data, preferred_element_type=jnp.float32)]
  transfers between devices with their start and end apart: 6 -> 0, of which waited for: 5 -> 0; matrix products, arithmetic and copies ran while one was open for 42% -> 0% of each run, Pallas kernels for 0% -> 0%
where the time goes in v1:
time: 155 us
  Pallas kernels  149 us (96%)
  local copies, waits for them, and re-layouts  5.41 us (3%)
    pallas_call x1, Pallas kernels, back(): pl.pallas_call(back_kernel, in_specs=[vmem] * 9, out_specs=[vmem] * 2, ou...  70.2 us
    pallas_call x1, Pallas kernels, mixer(): pl.pallas_call(mixer_kernel, in_specs=[pl.BlockSpec(memory_space=pltpu.VM...  54.7 us
    pallas_call x1, Pallas kernels, front(): pl.pallas_call(front_kernel, in_specs=[vmem] * 6, out_specs=[vmem] * 6, o...  24.2 us
    unnamed x2, local copies, waits for them, and re-layouts  4.13 us

profile of v1, /device:TPU:0, one launch (start us, length us, event | category | flops | bytes accessed | tf_op | source)
XLA Modules:
  0.0 155.1 jit_solution(2948480260220504258)
XLA Ops:
  0.6 1.3 dynamic_slice.3
  1.9 24.2 %front.1 = (bf16[3,64,2048]{2,1,0:T(8,128)(2,1)}, f32[2,64,2048]{2,1,0:T(8,128)}, f32[2,64,2048]{2,1,0:T(8,128)}, bf16[2,64,2048]{2,1,0:T(8,128)(2,1)}, bf16[3,6...) custom-call(bf16[1,64,6144]{2,1,0:T(8,128)(2,1)} %clean_ref.1, bf16[1,64,6144]{2,1,0:T(8,128)(2,1)} %pert_ref.1, ...), custom_call_target="tpu_custom_call" | custom-call | tf_op jit(solution)/shard_map/front/pallas_call | solution.py:596
  26.1 54.7 %mixer.1.slope_ref = f32[2,64,2048]{2,1,0:T(8,128)} custom-call(bf16[3,64,2048]{2,1,0:T(8,128)(2,1)} %get-tuple-element.8.prod_ref, bf16[2048,1024]{1,0:T(8,128)(2,1)} %weight_ref.1, f32[1,1024]{1,0:T(1,128)} %bitcast.7), custom_call_target="tpu_custom_call" | custom-call | tf_op jit(solution)/shard_map/mixer/pallas_call | solution.py:355
  80.8 70.2 %back.1 = (bf16[1,64,6144]{2,1,0:T(8,128)(2,1)}, bf16[1,64,6144]{2,1,0:T(8,128)(2,1)}) custom-call(f32[2,64,2048]{2,1,0:T(8,128)} %mixer.1.slope_ref, bf16[3,64,2048]{2,1,0:T(8,128)(2,1)} %get-tuple-element.9.query_ref, f32[2,64,2048]{2,1,0:T(8,128)} %get-tuple-element.10.key_ref, f32[2,64,2048]{2,1,0:T(8,128)} %get-tuple-element.11.value_ref, ...), custom_call_target="tpu_custom_call" | custom-call | tf_op jit(solution)/shard_map/back/pallas_call | solution.py:760
  151.0 2.1 %copy.12 = bf16[1,64,6144]{2,1,0:T(8,128)(2,1)} copy(bf16[1,64,6144]{2,1,0:T(8,128)(2,1)} %get-tuple-element.16) | data formatting | bytes 1572864
  153.0 2.1 %copy.13 = bf16[1,64,6144]{2,1,0:T(8,128)(2,1)} copy(bf16[1,64,6144]{2,1,0:T(8,128)(2,1)} %get-tuple-element.17) | data formatting | bytes 1572864

commit v2 on v0

v2 whole, which is shorter than its diff:
```python
import math

import jax
import jax.numpy as jnp
from jax import lax
from jax.experimental import pallas as pl
from jax.experimental.pallas import tpu as pltpu
from jax.sharding import PartitionSpec as P

eps = 1e-06
teacher_weight = 0.5
f32 = jnp.float32
bf16 = jnp.bfloat16
LANES = 128
SUB = 8


def row_index():
    return lax.broadcasted_iota(jnp.int32, (SUB, LANES), 0).astype(f32)


def split_rows(value):
    return [value[SUB * i : SUB * (i + 1)] for i in range(value.shape[0] // SUB)]


def shifted_down(value, steps):
    if steps == 0:
        return value
    rows = lax.broadcasted_iota(jnp.int32, value.shape, 0)
    return jnp.where(rows >= steps, pltpu.roll(value, steps, 0), 0.0)


def shifted_up(value, steps):
    if steps == 0:
        return value
    count = value.shape[0]
    rows = lax.broadcasted_iota(jnp.int32, value.shape, 0)
    return jnp.where(rows < count - steps, pltpu.roll(value, count - steps, 0), 0.0)


def filter_table(res, rate, rows):
    row = row_index()
    tiles = [jnp.zeros((SUB, LANES), f32) for _ in range(rows // SUB)]
    for m in range(res.shape[0]):
        current = res[m : m + 1] * jnp.exp(-rate[m : m + 1] * row)
        step = jnp.exp(-rate[m : m + 1] * SUB)
        for i in range(len(tiles)):
            tiles[i] = tiles[i] + current
            current = current * step
    return jnp.concatenate(tiles, 0)


def direct_conv(value, table_row, causal):
    count = value.shape[0] // SUB
    out = [jnp.zeros((SUB, LANES), f32) for _ in range(count)]
    for b in range(SUB):
        tiles = split_rows(shifted_down(value, b) if causal else shifted_up(value, b))
        for a in range(count):
            weight = jnp.broadcast_to(table_row(SUB * a + b), (SUB, LANES))
            for i in range(count - a):
                if causal:
                    out[i + a] = out[i + a] + weight * tiles[i]
                else:
                    out[i] = out[i] + weight * tiles[i + a]
    return jnp.concatenate(out, 0)


def block_states(values, rate, causal, store):
    row = row_index()
    split = [split_rows(value) for value in values]
    count = len(split[0])
    for m in range(rate.shape[0]):
        one = rate[m : m + 1]
        step = jnp.exp(-one * SUB)
        if causal:
            current, order = jnp.exp(-one * (SUB - 1.0 - row)), range(count - 1, -1, -1)
        else:
            current, order = jnp.exp(-one * row), range(count)
        sums = [jnp.zeros((SUB, LANES), f32) for _ in split]
        for place, i in enumerate(order):
            sums = [total + current * tiles[i] for total, tiles in zip(sums, split)]
            if place < count - 1:
                current = current * step
        for s, total in enumerate(sums):
            store(s, m, jnp.sum(total, 0, keepdims=True))


def reached(locals_, state_row, res, rate, causal):
    row = row_index()
    split = [split_rows(value) for value in locals_]
    count = len(split[0])
    for m in range(rate.shape[0]):
        one = rate[m : m + 1]
        step = jnp.exp(-one * SUB)
        if causal:
            current, order = res[m : m + 1] * jnp.exp(-one * (row + 1.0)), range(count)
        else:
            current, order = res[m : m + 1] * jnp.exp(-one * (SUB - row)), range(count - 1, -1, -1)
        states = [jnp.broadcast_to(state_row(s, m), (SUB, LANES)) for s in range(len(split))]
        for place, i in enumerate(order):
            for s, tiles in enumerate(split):
                tiles[i] = tiles[i] + current * states[s]
            if place < count - 1:
                current = current * step
    return [jnp.concatenate(tiles, 0) for tiles in split]


def lane_loop(width, body):
    def step(i, carry):
        body(pl.ds(pl.multiple_of(i * LANES, LANES), LANES))
        return carry

    lax.fori_loop(0, width // LANES, step, 0)


MESH = pl.DeviceIdType.MESH


def remote(axis, source, target, send, recv, peer):
    return pltpu.make_async_remote_copy(
        src_ref=source,
        dst_ref=target,
        send_sem=send,
        recv_sem=recv,
        device_id={axis: peer},
        device_id_type=MESH,
    )


def dp_peers():
    me = lax.axis_index("dp")
    chip, core = me // 2, me % 2
    sibling = chip * 2 + (1 - core)
    across = (1 - chip) * 2 + core
    diagonal = (1 - chip) * 2 + (1 - core)
    return me, sibling, across, diagonal


def mixer_grads_kernel(
    clean_ref,
    pert_ref,
    teacher_ref,
    tap_ref,
    res_ref,
    rate_ref,
    gain_ref,
    weight_hbm,
    grad_clean_ref,
    grad_pert_ref,
    weight_ref,
    query_ref,
    key_ref,
    value_ref,
    conv_ref,
    prod_ref,
    table_ref,
    gated_ref,
    slope_ref,
    local_ref,
    tail_ref,
    halo_out,
    halo_in,
    head_out,
    head_in,
    going_ref,
    coming_ref,
    back_going_ref,
    back_coming_ref,
    rows_ref,
    y_ref,
    tile_ref,
    sums_ref,
    out_ref,
    hold_ref,
    send_ref,
    land_ref,
    weight_sem,
    halo_sem,
    head_sem,
    chain_send,
    chain_recv,
    back_chain_send,
    back_chain_recv,
    row_send,
    row_recv,
    sum_send,
    sum_recv,
    part_send,
    part_recv,
):
    feats = (clean_ref, pert_ref, teacher_ref)
    grads = (grad_clean_ref, grad_pert_ref)
    rows, width = clean_ref.shape[1], clean_ref.shape[2] // 3
    own_width = weight_ref.shape[1]
    full_width = own_width * lax.axis_size("dp")
    pieces = part_send.shape[1]
    piece = width // pieces
    links = chain_send.shape[0]
    link = width // links
    links_each = links // pieces
    here, count = lax.axis_index("ctx"), lax.axis_size("ctx")
    after, before = lax.rem(here + 1, count), lax.rem(here + count - 1, count)
    at_start, at_end = here == 0, here == count - 1
    inside_start, inside_end = here > 0, here < count - 1
    upper = here >= count // 2
    lower = here < count // 2
    me, sibling, across, diagonal = dp_peers()

    def span_of(c):
        return pl.ds(c * piece, piece)

    def piece_loop(c, body):
        def step(i, carry):
            body(pl.multiple_of(c * piece + i * LANES, LANES))
            return carry

        lax.fori_loop(0, piece // LANES, step, 0)

    def lanes_at(first):
        return pl.ds(pl.multiple_of(first, LANES), LANES)

    weight_copy = pltpu.make_async_copy(weight_hbm, weight_ref, weight_sem.at[0])
    weight_copy.start()

    barrier = pltpu.get_barrier_semaphore()
    for peer in (after, before):
        pl.semaphore_signal(barrier, inc=1, device_id={"ctx": peer}, device_id_type=MESH)
    for peer in (sibling, across, diagonal):
        pl.semaphore_signal(barrier, inc=1, device_id={"dp": peer}, device_id_type=MESH)

    def tails(lanes):
        kept = [f[0, rows - 16 :, lanes].astype(f32)[14:] for f in feats]
        halo_out[:, lanes] = jnp.concatenate(kept + [jnp.zeros((2, LANES), f32)], 0)

    lane_loop(3 * width, tails)
    pl.semaphore_wait(barrier, 5)
    halo = remote("ctx", halo_out, halo_in, halo_sem.at[0], halo_sem.at[1], after)

    @pl.when(inside_end)
    def _():
        halo.start()

    def tables(lanes):
        table_ref[:, lanes] = filter_table(res_ref[:, lanes], rate_ref[:, lanes], rows)

    lane_loop(width, tables)

    @pl.when(at_start)
    def _():
        halo_in[...] = jnp.zeros(halo_in.shape, f32)

    @pl.when(inside_start)
    def _():
        halo.wait_recv()

    def filtered(s, lanes):
        row = lax.broadcasted_iota(jnp.int32, (rows, LANES), 0)
        now = feats[s][0, :, lanes].astype(f32)
        back_two, back_one = halo_in[2 * s : 2 * s + 1, lanes], halo_in[2 * s + 1 : 2 * s + 2, lanes]
        one = jnp.where(row >= 1, pltpu.roll(now, 1, 0), back_one)
        two = jnp.where(row >= 2, pltpu.roll(now, 2, 0), jnp.where(row == 1, back_one, back_two))
        return tap_ref[0:1, lanes] * now + tap_ref[1:2, lanes] * one + tap_ref[2:3, lanes] * two

    def features(first):
        lanes, klanes, vlanes = [lanes_at(first + j * width) for j in range(3)]
        gated = []
        for s in range(3):
            query_ref[s, :, lanes] = filtered(s, lanes).astype(bf16)
            k, v = filtered(s, klanes), filtered(s, vlanes)
            if s < 2:
                key_ref[s, :, lanes] = k
                value_ref[s, :, lanes] = v
            gated.append((k * v).astype(bf16).astype(f32))
            gated_ref[s, :, lanes] = gated[s]

        def store(s, m, value):
            going_ref[s, pl.ds(m, 1), lanes] = value

        block_states(gated, rate_ref[:, lanes], True, store)

    def link_of(c):
        return pl.ds(c * link, link)

    def pass_on(c, going, coming, copies, is_first, inside_first, inside_last):
        @pl.when(is_first)
        def _():
            coming[:, :, link_of(c)] = jnp.zeros((coming.shape[0], coming.shape[1], link), f32)

        @pl.when(inside_first)
        def _():
            copies[c].wait_recv()

        @pl.when(inside_last)
        def _():
            lanes = link_of(c)
            decay = jnp.exp(-rate_ref[:, lanes] * rows)
            for s in range(going.shape[0]):
                going[s, :, lanes] = going[s, :, lanes] + decay * coming[s, :, lanes]
            copies[c].start()

    def chain(going, coming, send, recv, peer):
        return [
            remote(
                "ctx",
                going.at[:, :, link_of(c)],
                coming.at[:, :, link_of(c)],
                send.at[c],
                recv.at[c],
                peer,
            )
            for c in range(links)
        ]

    forward_chain = chain(going_ref, coming_ref, chain_send, chain_recv, after)
    backward_chain = chain(back_going_ref, back_coming_ref, back_chain_send, back_chain_recv, before)

    def direct(first):
        lanes = lanes_at(first)
        for s in range(3):
            gated_ref[s, :, lanes] = direct_conv(
                gated_ref[s, :, lanes], lambda j: table_ref[pl.ds(j, 1), lanes], True
            )

    def finish(first):
        lanes = lanes_at(first)
        full = reached(
            [gated_ref[s, :, lanes] for s in range(3)],
            lambda s, m: coming_ref[s, pl.ds(m, 1), lanes],
            res_ref[:, lanes],
            rate_ref[:, lanes],
            True,
        )
        for s in range(3):
            conv = full[s].astype(bf16)
            if s < 2:
                conv_ref[s, :, lanes] = conv
            prod_ref[s * rows : (s + 1) * rows, lanes] = (
                query_ref[s, :, lanes].astype(f32) * conv.astype(f32)
            ).astype(bf16)

    def row_copy(slot, c):
        source = rows_ref.at[1] if slot == 2 else prod_ref
        return remote(
            "dp",
            source.at[:, span_of(c)],
            rows_ref.at[slot, :, span_of(c)],
            row_send.at[slot, c],
            row_recv.at[slot, c],
            across if slot == 1 else sibling,
        )

    row_copies = [[row_copy(slot, c) for c in range(pieces)] for slot in range(3)]

    def forward_pass(c):
        for n in range(c * links_each, (c + 1) * links_each):
            pass_on(n, going_ref, coming_ref, forward_chain, at_start, inside_start, inside_end)

    for c in range(pieces):
        piece_loop(c, features)

    @pl.when(upper)
    def _():
        for c in range(pieces):
            piece_loop(c, direct)
        for c in range(pieces):
            forward_pass(c)
            piece_loop(c, finish)
            row_copies[1][c].start()
            row_copies[0][c].start()

    @pl.when(lower)
    def _():
        for c in range(pieces):
            forward_pass(c)
        for c in range(pieces):
            piece_loop(c, direct)
            piece_loop(c, finish)
            row_copies[1][c].start()
            row_copies[0][c].start()

    weight_copy.wait()
    tile = min(256, own_width)

    def project(source, place, c):
        def step(i, carry):
            lanes = pl.ds(pl.multiple_of(i * tile, tile), tile)
            part = jnp.dot(source(), weight_ref[span_of(c), lanes], preferred_element_type=f32)
            y_ref[place, :, lanes] = part if c == 0 else y_ref[place, :, lanes] + part
            return carry

        lax.fori_loop(0, own_width // tile, step, 0)

    def add_up(place):
        lane = lax.broadcasted_iota(jnp.int32, (SUB, LANES), 1)

        def step(i, carry):
            first = pl.multiple_of(i * SUB, SUB)
            yc, yp, yt = [y_ref[place, pl.ds(first + s * rows, SUB), :] for s in range(3)]
            gc, gp, gt = [gain_ref[...] * y for y in (yc, yp, yt)]
            pairs = ((yc, yc), (yp, yp), (yt, yt), (gc, gc), (gp, gp), (gc, gp), (gp, gt))
            result = jnp.zeros((SUB, LANES), f32)
            for n, (a, b) in enumerate(pairs):
                result = jnp.where(lane == n, jnp.sum(a * b, 1, keepdims=True), result)
            tile_ref[pl.ds(pl.multiple_of(place * rows + first, SUB), SUB), :] = result
            return carry

        lax.fori_loop(0, rows // SUB, step, 0)

    for c in range(pieces):
        project(lambda: prod_ref[:, span_of(c)], 0, c)
    add_up(0)
    for c in range(pieces):
        row_copies[1][c].wait_recv()
        row_copies[2][c].start()
        row_copies[0][c].wait_recv()
        project(lambda: rows_ref[0, :, span_of(c)], 1, c)
        project(lambda: rows_ref[1, :, span_of(c)], 2, c)
        if c > 0:
            row_copies[2][c - 1].wait_recv()
            project(lambda: rows_ref[2, :, span_of(c - 1)], 3, c - 1)
    add_up(1)
    add_up(2)
    row_copies[2][pieces - 1].wait_recv()
    project(lambda: rows_ref[2, :, span_of(pieces - 1)], 3, pieces - 1)
    add_up(3)

    packed = tile_ref[...].T[:SUB]
    owners = (me, sibling, across, diagonal)
    for place, owner in enumerate(owners):
        sums_ref[me, owner] = packed[:, place * rows : (place + 1) * rows]
    exchanged = [
        remote("dp", sums_ref.at[me], sums_ref.at[me], sum_send.at[n], sum_recv.at[n], peer)
        for n, peer in enumerate((sibling, across, diagonal))
    ]
    for one in exchanged:
        one.start()
    for one in exchanged:
        one.wait()
    sums_ref[me] = sums_ref[0] + sums_ref[1] + sums_ref[2] + sums_ref[3]
    for place, owner in enumerate(owners):
        columns = jnp.concatenate([sums_ref[me, owner], jnp.zeros((LANES - SUB, rows), f32)], 0)
        tile_ref[place * rows : (place + 1) * rows, :] = columns.T

    def slopes(place):
        high = 16

        def step(i, carry):
            first = pl.multiple_of(i * high, high)
            yc, yp, yt = [y_ref[place, pl.ds(first + s * rows, high), :] for s in range(3)]
            sums = tile_ref[pl.ds(pl.multiple_of(place * rows + first, high), high), :]
            inv_c, inv_p, inv_t = [
                lax.rsqrt(sums[:, n : n + 1] / full_width + eps) for n in range(3)
            ]
            cc, pp, cp, pt = [sums[:, n : n + 1] for n in range(3, 7)]
            inner_c = -2.0 * (inv_p * cp - inv_c * cc)
            inner_p = 2.0 * (inv_p * pp - inv_c * cp) + 2.0 * teacher_weight * (
                inv_p * pp - inv_t * pt
            )
            gain = gain_ref[...]
            nc, np_, nt = yc * inv_c * gain, yp * inv_p * gain, yt * inv_t * gain
            change = np_ - nc
            slope_c = -2.0 * change
            slope_p = 2.0 * change + 2.0 * teacher_weight * (np_ - nt)
            out_c = inv_c * gain * slope_c - yc * (inv_c * inv_c * inv_c * (inner_c / full_width))
            out_p = inv_p * gain * slope_p - yp * (inv_p * inv_p * inv_p * (inner_p / full_width))
            out_ref[place, pl.ds(first, high), :] = out_c.astype(bf16)
            out_ref[place, pl.ds(pl.multiple_of(rows + first, high), high), :] = out_p.astype(bf16)
            return carry

        lax.fori_loop(0, rows // high, step, 0)

    wide = math.gcd(piece, 256)

    def pull(place, c, store):
        def step(i, carry):
            lanes = pl.ds(pl.multiple_of(c * piece + i * wide, wide), wide)
            store(
                lanes,
                lax.dot_general(
                    out_ref[place],
                    weight_ref[lanes, :],
                    (((1,), (1,)), ((), ())),
                    preferred_element_type=f32,
                ),
            )
            return carry

        lax.fori_loop(0, piece // wide, step, 0)

    def to_send(slot):
        def store(lanes, value):
            send_ref[slot, :, lanes] = value.astype(bf16)

        return store

    def to_hold(lanes, value):
        hold_ref[:, lanes] = value

    parts = [
        [
            remote(
                "dp",
                send_ref.at[n, :, span_of(c)],
                land_ref.at[n, :, span_of(c)],
                part_send.at[n, c],
                part_recv.at[n, c],
                across if n == 1 else sibling,
            )
            for c in range(pieces)
        ]
        for n in range(3)
    ]

    def join(c):
        parts[0][c].wait_recv()

        def step(first):
            lanes = lanes_at(first)
            send_ref[1, :, lanes] = (
                hold_ref[:, lanes] + land_ref[0, :, lanes].astype(f32)
            ).astype(bf16)

        piece_loop(c, step)
        parts[1][c].start()

    slopes(3)
    slopes(2)
    for c in range(pieces):
        pull(3, c, to_send(0))
        parts[0][c].start()
        pull(2, c, to_hold)
        if c > 0:
            join(c - 1)
    join(pieces - 1)
    slopes(1)
    for c in range(pieces):
        pull(1, c, to_send(2))
        parts[2][c].start()
    slopes(0)
    for c in range(pieces):
        pull(0, c, to_hold)

    def conv_slopes(first):
        lanes = lanes_at(first)
        total = (
            hold_ref[:, lanes]
            + land_ref[2, :, lanes].astype(f32)
            + land_ref[1, :, lanes].astype(f32)
        )
        values = []
        for s in range(2):
            own = total[s * rows : (s + 1) * rows]
            slope_ref[s, :, lanes] = own * conv_ref[s, :, lanes].astype(f32)
            values.append((own * query_ref[s, :, lanes].astype(f32)).astype(bf16).astype(f32))
            local_ref[s, :, lanes] = values[s]

        def store(s, m, value):
            back_going_ref[s, pl.ds(m, 1), lanes] = value

        block_states(values, rate_ref[:, lanes], False, store)

    def back_direct(first):
        lanes = lanes_at(first)
        for s in range(2):
            local_ref[s, :, lanes] = direct_conv(
                local_ref[s, :, lanes], lambda j: table_ref[pl.ds(j, 1), lanes], False
            )

    def backward_pass(c):
        for n in range(c * links_each, (c + 1) * links_each):
            pass_on(
                n, back_going_ref, back_coming_ref, backward_chain, at_end, inside_end, inside_start
            )

    def tapped(unit, lanes, next_one, next_two):
        high = unit.shape[0]
        row = lax.broadcasted_iota(jnp.int32, unit.shape, 0)
        one = jnp.where(row < high - 1, pltpu.roll(unit, high - 1, 0), next_one)
        two = jnp.where(
            row < high - 2,
            pltpu.roll(unit, high - 2, 0),
            jnp.where(row == high - 2, next_one, next_two),
        )
        return (
            tap_ref[0:1, lanes] * unit + tap_ref[1:2, lanes] * one + tap_ref[2:3, lanes] * two
        ).astype(bf16)

    def units(first):
        places = [lanes_at(first + j * width) for j in range(3)]
        lanes = places[0]
        full = reached(
            [local_ref[s, :, lanes] for s in range(2)],
            lambda s, m: back_coming_ref[s, pl.ds(m, 1), lanes],
            res_ref[:, lanes],
            rate_ref[:, lanes],
            False,
        )
        none = jnp.zeros((1, LANES), f32)
        for j, place in enumerate(places):
            firsts = []
            for s in range(2):
                if j == 0:
                    unit = slope_ref[s, :, lanes]
                else:
                    other = value_ref if j == 1 else key_ref
                    unit = full[s].astype(bf16).astype(f32) * other[s, :, lanes]
                firsts.append(unit[:2])
                tail_ref[s, :, place] = unit[rows - 16 :]
                grads[s][0, :, place] = tapped(unit, place, none, none)
            head_out[:, place] = jnp.concatenate(firsts + [jnp.zeros((4, LANES), f32)], 0)

    def arrive(c):
        parts[2][c].wait_recv()
        parts[1][c].wait_recv()
        piece_loop(c, conv_slopes)

    @pl.when(upper)
    def _():
        for c in range(pieces):
            arrive(c)
            backward_pass(c)
        for c in range(pieces):
            piece_loop(c, back_direct)
            piece_loop(c, units)

    @pl.when(lower)
    def _():
        for c in range(pieces):
            arrive(c)
            piece_loop(c, back_direct)
        for c in range(pieces):
            backward_pass(c)
            piece_loop(c, units)

    head = remote("ctx", head_out, head_in, head_sem.at[0], head_sem.at[1], before)

    @pl.when(inside_start)
    def _():
        head.start()

    @pl.when(inside_end)
    def _():
        head.wait_recv()

        def mend(lanes):
            for s in range(2):
                grads[s][0, rows - 16 :, lanes] = tapped(
                    tail_ref[s, :, lanes],
                    lanes,
                    head_in[2 * s : 2 * s + 1, lanes],
                    head_in[2 * s + 1 : 2 * s + 2, lanes],
                )

        lane_loop(3 * width, mend)

    for group in row_copies + parts:
        for one in group:
            one.wait_send()

    @pl.when(inside_end)
    def _():
        halo.wait_send()
        for one in forward_chain:
            one.wait_send()

    @pl.when(inside_start)
    def _():
        head.wait_send()
        for one in backward_chain:
            one.wait_send()


def mixer_grads(feats, taps, res, rate, gain, weight):
    _, rows, width3 = feats[0].shape
    width, modes, own_width = width3 // 3, res.shape[0], weight.shape[1]
    pieces, links = math.gcd(width // LANES, 4), math.gcd(width // LANES, 16)
    vmem = pl.BlockSpec(memory_space=pltpu.VMEM)
    dma = pltpu.SemaphoreType.DMA
    return pl.pallas_call(
        mixer_grads_kernel,
        in_specs=[vmem] * 7 + [pl.BlockSpec(memory_space=pl.ANY)],
        out_specs=[vmem] * 2,
        out_shape=[jax.ShapeDtypeStruct((1, rows, width3), bf16)] * 2,
        scratch_shapes=[
            pltpu.VMEM(weight.shape, bf16),
            pltpu.VMEM((3, rows, width), bf16),
            pltpu.VMEM((2, rows, width), f32),
            pltpu.VMEM((2, rows, width), f32),
            pltpu.VMEM((2, rows, width), bf16),
            pltpu.VMEM((3 * rows, width), bf16),
            pltpu.VMEM((rows, width), f32),
            pltpu.VMEM((3, rows, width), f32),
            pltpu.VMEM((2, rows, width), f32),
            pltpu.VMEM((2, rows, width), f32),
            pltpu.VMEM((2, 16, width3), f32),
            pltpu.VMEM((SUB, width3), f32),
            pltpu.VMEM((SUB, width3), f32),
            pltpu.VMEM((SUB, width3), f32),
            pltpu.VMEM((SUB, width3), f32),
            pltpu.VMEM((3, modes, width), f32),
            pltpu.VMEM((3, modes, width), f32),
            pltpu.VMEM((2, modes, width), f32),
            pltpu.VMEM((2, modes, width), f32),
            pltpu.VMEM((3, 3 * rows, width), bf16),
            pltpu.VMEM((4, 3 * rows, own_width), f32),
            pltpu.VMEM((4 * rows, LANES), f32),
            pltpu.VMEM((4, 4, SUB, rows), f32),
            pltpu.VMEM((4, 2 * rows, own_width), bf16),
            pltpu.VMEM((2 * rows, width), f32),
            pltpu.VMEM((3, 2 * rows, width), bf16),
            pltpu.VMEM((3, 2 * rows, width), bf16),
            dma((1,)),
            dma((2,)),
            dma((2,)),
            dma((links,)),
            dma((links,)),
            dma((links,)),
            dma((links,)),
            dma((3, pieces)),
            dma((3, pieces)),
            dma((3,)),
            dma((3,)),
            dma((3, pieces)),
            dma((3, pieces)),
        ],
        compiler_params=pltpu.CompilerParams(
            collective_id=0, has_side_effects=True, vmem_limit_bytes=60 * 2**20
        ),
        name="mixer_grads",
    )(*feats, taps, res, rate, gain, weight)


def per_device(
    feat_clean, feat_pert, feat_teacher, short_taps, residues, decay_rate, out_weight, norm_gain
):
    own_width = out_weight.shape[1]
    gain = lax.dynamic_slice_in_dim(norm_gain, lax.axis_index("dp") * own_width, own_width, 0)
    return mixer_grads(
        (feat_clean, feat_pert, feat_teacher),
        short_taps,
        residues.T,
        decay_rate.T,
        gain[None],
        out_weight,
    )


def solution(mesh):
    in_specs = (
        P("dp", "ctx", None),
        P("dp", "ctx", None),
        P("dp", "ctx", None),
        P(),
        P(),
        P(),
        P(None, "dp"),
        P(),
    )
    out_specs = (P("dp", "ctx", None), P("dp", "ctx", None))
    return jax.shard_map(
        per_device, mesh=mesh, in_specs=in_specs, out_specs=out_specs, check_vma=False
    )
```

time: 828 us -> 120 us (0.14)
  local copies, waits for them, and re-layouts: 545 us -> 5.41 us
  matrix products: 151 us -> 0 us
  Pallas kernels: 0 us -> 114 us
  waiting for transfers between devices: 63.6 us -> 0 us
  starting transfers between devices: 21.1 us -> 0 us
  blocking collectives: 18.1 us -> 0 us
  between operations: 14.8 us -> 0.64 us
  other arithmetic: 9.11 us -> 0 us
    gather x16 -> x0, local copies, waits for them, and re-layouts: 495 us -> none  [modal_group(): jnp.take(kernel, jnp.clip(offset, 0, block - 1), axis=1)]
    dot_general x58 -> x0, matrix products: 151 us -> none  [the longest x8 60.2 us: modal_group(): jnp.einsum('gmab,sgbm->sgam', carry_map, block_ends, precision=highest)]
    pallas_call x0 -> x1, Pallas kernels: none -> 114 us  [mixer_grads(): pl.pallas_call(mixer_grads_kernel, in_specs=[vmem] * 7 + [pl.BlockSpec(me...]
    all_to_all x3 -> x0, waiting for transfers between devices: 56.4 us -> none  [the longest x1 23.7 us: per_device(): lax.all_to_all(result.astype(jnp.bfloat16), 'ctx', split_axis=2, concat_a...]
    all_to_all x1 -> x0, blocking collectives: 18.1 us -> none  [per_device(): lax.all_to_all(jnp.flip(result, 2).astype(jnp.bfloat16), 'ctx', split_axi...]
    all_to_all x3 -> x0, starting transfers between devices: 14.9 us -> none  [the longest x1 6.68 us: per_device(): lax.all_to_all(gated, 'ctx', split_axis=1, concat_axis=2, tiled=True)]
    add x8 -> x0, local copies, waits for them, and re-layouts: 9.25 us -> none  [split_product(): jnp.einsum(form, upper, data, preferred_element_type=jnp.float32)]
  transfers between devices with their start and end apart: 6 -> 0, of which waited for: 5 -> 0; matrix products, arithmetic and copies ran while one was open for 42% -> 0% of each run, Pallas kernels for 0% -> 0%
where the time goes in v2:
time: 120 us
  Pallas kernels  114 us (95%)
  local copies, waits for them, and re-layouts  5.41 us (5%)
    pallas_call x1, Pallas kernels, mixer_grads(): pl.pallas_call(mixer_grads_kernel, in_specs=[vmem] * 7 + [pl.BlockSpec(me...  114 us
    unnamed x2, local copies, waits for them, and re-layouts  4.13 us

profile of v2, /device:TPU:0, one launch (start us, length us, event | category | flops | bytes accessed | tf_op | source)
XLA Modules:
  0.0 120.2 jit_solution(15303265417531037755)
XLA Ops:
  0.6 1.3 %dynamic_slice.3 = f32[1024]{0:T(1024)} dynamic-slice(f32[4096]{0:T(1024)} %param.15, s32[]{:T(128)S(6)} %select_n.3), dynamic_slice_sizes={1024} | dynamic-slice | bytes 8196 | tf_op jit(solution)/shard_map/dynamic_slice | solution.py:737
  1.9 114.2 %mixer_grads.1 = (bf16[1,64,6144]{2,1,0:T(8,128)(2,1)}, bf16[1,64,6144]{2,1,0:T(8,128)(2,1)}) custom-call(bf16[1,64,6144]{2,1,0:T(8,128)(2,1)} %clean_ref.1, bf16[1,64,6144]{2,1,0:T(8,128)(2,1)} %pert_ref.1, bf16[1,64,6144]{2,1,0:T(8,128)(2,1)} %teacher_ref.1, f32[3,6144]{1,0:T(4,128)} %tap_ref.1, f32[16,2048]{1,0:T(8,128)} %bitcast.3, f32[16,2048]{1,0:T(8,128)} %bitcast.4, ...), custom_call_target="tpu_custom_call" | custom-call | tf_op jit(solution)/shard_map/mixer_grads/pallas_call | solution.py:679
  116.1 2.1 %copy.12 = bf16[1,64,6144]{2,1,0:T(8,128)(2,1)} copy(bf16[1,64,6144]{2,1,0:T(8,128)(2,1)} %get-tuple-element.4) | data formatting | bytes 1572864
  118.2 2.1 %copy.13 = bf16[1,64,6144]{2,1,0:T(8,128)(2,1)} copy(bf16[1,64,6144]{2,1,0:T(8,128)(2,1)} %get-tuple-element.5) | data formatting | bytes 1572864
